TPU v7x, 32 devices: a whole 2x2x4 slice. The times are simulated.
32 devices in a mesh: leaf: 8 (over z, x), row: 4 (over y, core).
Axes of the slice: x: 2, y: 2, z: 4, core: 2. Of those that a mesh axis runs over, the one named last changes fastest.
Arguments:
- sec_rhs: float32 [64, 4096], P(None, ('leaf', 'row')), may hold values from -6 to 6
- sec_inverse: float32 [4096, 512], P(('leaf', 'row')), as said below
- sep_rhs: float32 [4, 64, 1024], P(None, None, 'leaf'), may hold values from -6 to 6
- sep_inverse: float32 [4, 1024, 1024], P(None, 'leaf'), as said below
- sep_coupling: float32 [3, 1024, 1024], P(None, 'leaf'), may hold values from -0.1875 to 0.1875
- sec_update: float32 [4, 1024, 4096], P(None, None, ('leaf', 'row')), may hold values from -0.1875 to 0.1875
- link: int32 [8, 4], P('leaf'), may hold values 0 or 1
Outputs:
- sec_solution: float32 [64, 4096], P(None, ('leaf', 'row'))
- sep_solution: float32 [4, 64, 1024], P(None, None, 'leaf')
Inputs may be any that keep to these rules, and one draw needn't show every extreme that they name: link holds only 0 and 1. Each section's block of sec_inverse is lower triangular with entries on the diagonal between 0.7 and 1.3. Each block of sep_inverse is lower triangular with entries on the diagonal between 0.7 and 1.3.
All inputs are finite; a program needn't handle non-finite values. No bound on the sum of `link` on one device may be relied on, other than what follows from the above.
Results may differ from a plain program's by a relative error of at most 0.00013.
Values sent between devices are 32-bit elements; how exact they have to be, the bound alone decides.
A program may use at most 128 MiB of HBM per device.

v0:
```python
import jax
import jax.numpy as jnp
from jax import lax
from jax.sharding import PartitionSpec as P


def dot_last(left, right):
    return lax.dot_general(
        left,
        right,
        (((1,), (1,)), ((), ())),
        precision=lax.Precision.HIGHEST,
        preferred_element_type=jnp.float32,
    )


def dot_plain(left, right):
    return jnp.dot(left, right, precision=lax.Precision.HIGHEST, preferred_element_type=jnp.float32)


def per_device(sec_rhs, sec_inverse, sep_rhs, sep_inverse, sep_coupling, sec_update, link):
    highest = lax.Precision.HIGHEST
    levels = sep_rhs.shape[0]
    link_weights = link[0].astype(jnp.float32)
    rhs_full = lax.all_gather(sec_rhs, "row", axis=1, tiled=True)
    y_sec = dot_last(rhs_full, sec_inverse)
    section_parts = (
        jnp.einsum("rj,kmj->krm", y_sec, sec_update, precision=highest)
        * link_weights[:, None, None]
    )
    row_total = lax.psum(section_parts, "row")
    reduced = lax.psum_scatter(row_total, "leaf", scatter_dimension=2, tiled=True)
    y_leaf = []
    y_full = None
    for level in range(levels):
        known_part = sep_rhs[level] - reduced[level]
        if level > 0:
            known_part = known_part - dot_last(y_full, sep_coupling[level - 1])
        known_full = lax.all_gather(known_part, "leaf", axis=1, tiled=True)
        y_level = dot_last(known_full, sep_inverse[level])
        y_leaf.append(y_level)
        if level < levels - 1:
            y_full = lax.all_gather(y_level, "leaf", axis=1, tiled=True)
    solved = [None] * levels
    rhs_width = y_leaf[0].shape[0] // lax.axis_size("row")
    rhs_start = lax.axis_index("row") * rhs_width
    for level in range(levels - 1, -1, -1):
        adjusted = lax.dynamic_slice_in_dim(y_leaf[level], rhs_start, rhs_width, 0)
        if level < levels - 1:
            coupling_part = dot_plain(solved[level + 1], sep_coupling[level])
            adjusted = adjusted - lax.psum_scatter(
                coupling_part, "leaf", scatter_dimension=1, tiled=True
            )
        solve_part = dot_plain(adjusted, sep_inverse[level])
        solved[level] = lax.psum_scatter(solve_part, "leaf", scatter_dimension=1, tiled=True)
    solved_stack = lax.all_gather(jnp.stack(solved), "row", axis=1, tiled=True)
    solved_full = lax.all_gather(solved_stack, "leaf", axis=2, tiled=True)
    weighted = solved_full * link_weights[:, None, None]
    back_sec = y_sec - jnp.einsum("krm,kmj->rj", weighted, sec_update, precision=highest)
    section_part = dot_plain(back_sec, sec_inverse)
    sec_solution = lax.psum_scatter(section_part, "row", scatter_dimension=1, tiled=True)
    return (sec_solution, solved_stack)


def solution(mesh):
    in_specs = (
        P(None, ("leaf", "row")),
        P(("leaf", "row"), None),
        P(None, None, "leaf"),
        P(None, "leaf", None),
        P(None, "leaf", None),
        P(None, None, ("leaf", "row")),
        P("leaf", None),
    )
    out_specs = (P(None, ("leaf", "row")), P(None, None, "leaf"))
    return jax.shard_map(
        per_device, mesh=mesh, in_specs=in_specs, out_specs=out_specs, check_vma=False
    )
```

profile of v0, /device:TPU:0, one launch (start us, length us, event | category | flops | bytes accessed | tf_op | source)
XLA Modules:
  0.0 811.1 jit_solution(3679977903072324729)
XLA Ops:
  7.2 6.9 all_gather.30
  14.1 0.7 convert_bitcast_fusion
  14.7 1.3 fusion.59
  16.1 3.3 fusion
  19.5 65.5 %reduce-scatter.26.cloned.1.call-done = f32[4,64,128]{2,1,0:T(8,128)} async-done(((f32[4,64,1024]{2,1,0:T(8,128)}), f32[4,64,128]{2,1,0:T(8,128)}) %reduce-scatter.26.cloned.1.call-update) | async-done | bytes 131088 | tf_op jit(solution)/shard_map/reduce_scatter | solution.py:32
  85.1 32.8 %all-reduce.2.cloned.1.call-done = f32[4,64,128]{2,1,0:T(8,128)} async-done(((f32[4,64,128]{2,1,0:T(8,128)}), f32[4,64,128]{2,1,0:T(8,128)}) %all-reduce.2.cloned.1.call-update) | async-done | bytes 131088 | tf_op jit(solution)/shard_map/psum | solution.py:31
  118.0 0.9 slice_subtract_fusion.3
  118.9 31.0 %all-gather = f32[1,64,1024]{2,1,0:T(8,128)S(1)} all-gather(f32[1,64,128]{2,1,0:T(8,128)S(1)} %slice_subtract_fusion.3), channel_id=2, replica_groups=mesh['leaf'=8,'row'=4] {'leaf'}, dimensions={2}, use_global_device_ids=true | all-gather | bytes 294912 | tf_op jit(solution)/shard_map/all_gather | solution.py:39
  149.9 1.7 fusion.26
  151.6 30.8 %all_gather.32 = f32[64,1024]{1,0:T(8,128)S(1)} all-gather(f32[64,128]{1,0:T(8,128)S(1)} %fusion.26), channel_id=1, replica_groups=mesh['leaf'=8,'row'=4] {'leaf'}, dimensions={1}, use_global_device_ids=true | all-gather | bytes 294912 | tf_op jit(solution)/shard_map/all_gather | solution.py:43
  182.4 1.7 convolution_subtract_fusion.2
  184.1 31.0 %all_gather.33 = f32[64,1024]{1,0:T(8,128)S(1)} all-gather(f32[64,128]{1,0:T(8,128)S(1)} %convolution_subtract_fusion.2), channel_id=1, replica_groups=mesh['leaf'=8,'row'=4] {'leaf'}, dimensions={1}, use_global_device_ids=true | all-gather | bytes 294912 | tf_op jit(solution)/shard_map/all_gather | solution.py:39
  215.1 0.7 fusion.19
  215.8 30.8 %all_gather.34 = f32[64,1024]{1,0:T(8,128)S(1)} all-gather(f32[64,128]{1,0:T(8,128)S(1)} %fusion.19), channel_id=1, replica_groups=mesh['leaf'=8,'row'=4] {'leaf'}, dimensions={1}, use_global_device_ids=true | all-gather | bytes 294912 | tf_op jit(solution)/shard_map/all_gather | solution.py:43
  246.5 1.4 convolution_subtract_fusion.1
  248.0 30.7 %all_gather.35 = f32[64,1024]{1,0:T(8,128)S(1)} all-gather(f32[64,128]{1,0:T(8,128)S(1)} %convolution_subtract_fusion.1), channel_id=1, replica_groups=mesh['leaf'=8,'row'=4] {'leaf'}, dimensions={1}, use_global_device_ids=true | all-gather | bytes 294912 | tf_op jit(solution)/shard_map/all_gather | solution.py:39
  278.7 0.7 fusion.12
  279.4 30.7 %all_gather.36 = f32[64,1024]{1,0:T(8,128)S(1)} all-gather(f32[64,128]{1,0:T(8,128)S(1)} %fusion.12), channel_id=1, replica_groups=mesh['leaf'=8,'row'=4] {'leaf'}, dimensions={1}, use_global_device_ids=true | all-gather | bytes 294912 | tf_op jit(solution)/shard_map/all_gather | solution.py:43
  310.1 1.4 convolution_subtract_fusion
  311.5 30.7 %all_gather.37 = f32[64,1024]{1,0:T(8,128)S(1)} all-gather(f32[64,128]{1,0:T(8,128)S(1)} %convolution_subtract_fusion), channel_id=1, replica_groups=mesh['leaf'=8,'row'=4] {'leaf'}, dimensions={1}, use_global_device_ids=true | all-gather | bytes 294912 | tf_op jit(solution)/shard_map/all_gather | solution.py:39
  342.3 0.7 fusion.5
  342.9 1.0 fusion.3
  344.0 53.8 %reduce-scatter.10.cloned.1.call-done = f32[16,128]{1,0:T(8,128)} async-done(((f32[16,1024]{1,0:T(8,128)}), f32[16,128]{1,0:T(8,128)}) %reduce-scatter.10.cloned.1.call-update) | async-done | bytes 8208 | tf_op jit(solution)/shard_map/reduce_scatter | solution.py:55
  397.8 2.1 fusion.7
  399.9 54.2 %reduce-scatter.12.cloned.1.call-done = f32[16,128]{1,0:T(8,128)} async-done(((f32[16,1024]{1,0:T(8,128)}), f32[16,128]{1,0:T(8,128)}) %reduce-scatter.12.cloned.1.call-update) | async-done | bytes 8208 | tf_op jit(solution)/shard_map/reduce_scatter | solution.py:51
  454.1 2.1 fusion.10
  456.2 0.0 reduce-scatter.16.cloned.1.call-start
  456.2 54.2 %reduce-scatter.14.cloned.1.call-done = f32[16,128]{1,0:T(8,128)} async-done(((f32[16,1024]{1,0:T(8,128)}), f32[16,128]{1,0:T(8,128)}) %reduce-scatter.14.cloned.1.call-update) | async-done | bytes 8208 | tf_op jit(solution)/shard_map/reduce_scatter | solution.py:55
  510.4 2.1 fusion.14
  512.5 0.0 reduce-scatter.18.cloned.1.call-start
  512.6 54.2 %reduce-scatter.16.cloned.1.call-done = f32[16,128]{1,0:T(8,128)} async-done(((f32[16,1024]{1,0:T(8,128)}), f32[16,128]{1,0:T(8,128)}) %reduce-scatter.16.cloned.1.call-update) | async-done | bytes 8208 | tf_op jit(solution)/shard_map/reduce_scatter | solution.py:51
  566.7 2.1 fusion.17
  568.8 0.0 reduce-scatter.20.cloned.1.call-start
  568.9 54.3 %reduce-scatter.18.cloned.1.call-done = f32[16,128]{1,0:T(8,128)} async-done(((f32[16,1024]{1,0:T(8,128)}), f32[16,128]{1,0:T(8,128)}) %reduce-scatter.18.cloned.1.call-update) | async-done | bytes 8208 | tf_op jit(solution)/shard_map/reduce_scatter | solution.py:55
  623.2 2.1 fusion.21
  625.3 0.0 reduce-scatter.22.cloned.1.call-start
  625.3 54.3 %reduce-scatter.20.cloned.1.call-done = f32[16,128]{1,0:T(8,128)} async-done(((f32[16,1024]{1,0:T(8,128)}), f32[16,128]{1,0:T(8,128)}) %reduce-scatter.20.cloned.1.call-update) | async-done | bytes 8208 | tf_op jit(solution)/shard_map/reduce_scatter | solution.py:51
  679.7 2.1 fusion.24
  681.7 0.0 all-gather.3.cloned.1.call-start
  681.8 54.4 %reduce-scatter.22.cloned.1.call-done = f32[16,128]{1,0:T(8,128)} async-done(((f32[16,1024]{1,0:T(8,128)}), f32[16,128]{1,0:T(8,128)}) %reduce-scatter.22.cloned.1.call-update) | async-done | bytes 8208 | tf_op jit(solution)/shard_map/reduce_scatter | solution.py:55
  736.2 0.7 pad_maximum_fusion
  736.9 5.9 all_gather.38
  742.8 0.0 reduce-scatter.24.cloned.1.call-start
  742.9 38.7 %all-gather.3.cloned.1.call-done = f32[4,64,1024]{2,1,0:T(8,128)} async-done(((f32[4,64,128]{2,1,0:T(8,128)}), f32[4,64,1024]{2,1,0:T(8,128)}) %all-gather.3.cloned.1.call-update) | async-done | bytes 1048592 | tf_op jit(solution)/shard_map/all_gather | solution.py:57
  781.6 2.7 fusion.1
  784.3 0.9 fusion.60
  785.2 18.6 %reduce-scatter.24.cloned.1.call-done = f32[64,128]{1,0:T(8,128)} async-done(((f32[64,512]{1,0:T(8,128)}), f32[64,128]{1,0:T(8,128)}) %reduce-scatter.24.cloned.1.call-update) | async-done | bytes 32784 | tf_op jit(solution)/shard_map/reduce_scatter | solution.py:61
  803.9 0.7 copy.11
  (32 shorter events, 0.4 us)
Async XLA Ops:
  7.2 8.9 %copy-start = (f32[4,1024,128]{2,1,0:T(8,128)S(1)}, f32[4,1024,128]{2,1,0:T(8,128)}, u32[]{:S(2)}) copy-start(f32[4,1024,128]{2,1,0:T(8,128)} %param.12) | copy-start | bytes 6291460
  7.2 77.9 %reduce-scatter.26.cloned.1.call-start = ((), (), s32[]{:S(2)}) async-start(), calls=%async_computation.18 | async-start | bytes 1179648 | tf_op jit(solution)/shard_map/reduce_scatter | solution.py:32
  16.1 101.9 %copy-start.5 = (f32[4,64,128]{2,1,0:T(8,128)S(1)}, f32[4,64,128]{2,1,0:T(8,128)}, u32[]{:S(2)}) copy-start(f32[4,64,128]{2,1,0:T(8,128)} %param.9) | copy-start | bytes 393220
  19.5 98.5 %all-reduce.2.cloned.1.call-start = ((), (), s32[]{:S(2)}) async-start(), calls=%async_computation.19 | async-start | bytes 262144 | tf_op jit(solution)/shard_map/psum | solution.py:31
  85.1 312.7 %reduce-scatter.10.cloned.1.call-start = ((), (), s32[]{:S(2)}) async-start(), calls=%async_computation.9 | async-start | bytes 73728 | tf_op jit(solution)/shard_map/reduce_scatter | solution.py:55
  118.0 97.2 %copy-start.1 = (f32[4,128,1024]{2,1,0:T(8,128)S(1)}, f32[4,128,1024]{2,1,0:T(8,128)}, u32[]{:S(2)}) copy-start(f32[4,128,1024]{2,1,0:T(8,128)} %param.10) | copy-start | bytes 6291460
  118.0 128.6 %copy-start.2 = (f32[3,128,1024]{2,1,0:T(8,128)S(1)}, f32[3,128,1024]{2,1,0:T(8,128)}, u32[]{:S(2)}) copy-start(f32[3,128,1024]{2,1,0:T(8,128)} %param.11) | copy-start | bytes 4718596
  344.0 110.2 %reduce-scatter.12.cloned.1.call-start = ((), (), s32[]{:S(2)}) async-start(), calls=%async_computation.10 | async-start | bytes 73728 | tf_op jit(solution)/shard_map/reduce_scatter | solution.py:51
  397.8 338.4 %copy-start.6 = (f32[16,128]{1,0:T(8,128)S(1)}, f32[16,128]{1,0:T(8,128)}, u32[]{:S(2)}) copy-start(f32[16,128]{1,0:T(8,128)} %reduce-scatter.10.cloned.1.call-done) | copy-start | bytes 24580
  399.9 110.5 %reduce-scatter.14.cloned.1.call-start = ((), (), s32[]{:S(2)}) async-start(), calls=%async_computation.11 | async-start | bytes 73728 | tf_op jit(solution)/shard_map/reduce_scatter | solution.py:55
  456.2 110.5 %reduce-scatter.16.cloned.1.call-start = ((), (), s32[]{:S(2)}) async-start(), calls=%async_computation.12 | async-start | bytes 73728 | tf_op jit(solution)/shard_map/reduce_scatter | solution.py:51
  510.4 225.8 %copy-start.7 = (f32[16,128]{1,0:T(8,128)S(1)}, f32[16,128]{1,0:T(8,128)}, u32[]{:S(2)}) copy-start(f32[16,128]{1,0:T(8,128)} %reduce-scatter.14.cloned.1.call-done) | copy-start | bytes 24580
  512.5 110.7 %reduce-scatter.18.cloned.1.call-start = ((), (), s32[]{:S(2)}) async-start(), calls=%async_computation.13 | async-start | bytes 73728 | tf_op jit(solution)/shard_map/reduce_scatter | solution.py:55
  568.8 110.8 %reduce-scatter.20.cloned.1.call-start = ((), (), s32[]{:S(2)}) async-start(), calls=%async_computation.14 | async-start | bytes 73728 | tf_op jit(solution)/shard_map/reduce_scatter | solution.py:51
  625.3 159.0 %copy-start.4 = (f32[128,512]{1,0:T(8,128)S(1)}, f32[128,512]{1,0:T(8,128)}, u32[]{:S(2)}) copy-start(f32[128,512]{1,0:T(8,128)} %param.8) | copy-start | bytes 786436
  625.3 110.9 %reduce-scatter.22.cloned.1.call-start = ((), (), s32[]{:S(2)}) async-start(), calls=%async_computation.15 | async-start | bytes 73728 | tf_op jit(solution)/shard_map/reduce_scatter | solution.py:55
  681.7 99.8 %all-gather.3.cloned.1.call-start = ((), (), s32[]{:S(2)}) async-start(), calls=%async_computation.16 | async-start | bytes 1179648 | tf_op jit(solution)/shard_map/all_gather | solution.py:57
  742.8 61.1 %copy-start.3 = (f32[4,64,128]{2,1,0:T(8,128)S(1)}, f32[4,64,128]{2,1,0:T(8,128)}, u32[]{:S(2)}) copy-start(f32[4,64,128]{2,1,0:T(8,128)} %all_gather.38) | copy-start | bytes 393220
  742.8 61.0 %reduce-scatter.24.cloned.1.call-start = ((), (), s32[]{:S(2)}) async-start(), calls=%async_computation.17 | async-start | bytes 163840 | tf_op jit(solution)/shard_map/reduce_scatter | solution.py:61
Sparse Core Ops, SparseCore 0:
  19.6 65.4 reduce-scatter.25
  87.5 30.4 all-reduce.1
  344.1 53.6 reduce-scatter.9
  401.4 52.7 reduce-scatter.11
  457.7 52.7 reduce-scatter.13
  514.0 52.7 reduce-scatter.15
  570.4 52.7 reduce-scatter.17
  626.9 52.7 reduce-scatter.19
  683.4 52.7 reduce-scatter.21
  742.9 38.5 all-gather.2
  785.4 18.4 reduce-scatter.23
where the time goes:
time: 812 us; the launch traced here: 811 us
  waiting for transfers between devices  535 us (66%)
  blocking collectives  229 us (28%)
  matrix products  29.9 us (4%)
  between operations  14 us (2%)
    reduce_scatter x4, waiting for transfers between devices, per_device(): lax.psum_scatter(solve_part, 'leaf', scatter_dimension=1, tiled=True)  217 us
    reduce_scatter x3, waiting for transfers between devices, per_device(): lax.psum_scatter(coupling_part, 'leaf', scatter_dimension=1, tiled=True)  163 us
    all_gather x4, blocking collectives, per_device(): known_full = lax.all_gather(known_part, 'leaf', axis=1, tiled=True)  123 us
    all_gather x3, blocking collectives, per_device(): y_full = lax.all_gather(y_level, 'leaf', axis=1, tiled=True)  92.3 us
    reduce_scatter x1, waiting for transfers between devices, per_device(): lax.psum_scatter(row_total, 'leaf', scatter_dimension=2, tiled=True)  65.5 us
    all_gather x1, waiting for transfers between devices, per_device(): solved_full = lax.all_gather(solved_stack, 'leaf', axis=2, tiled=True)  38.7 us
    psum x1, waiting for transfers between devices, per_device(): row_total = lax.psum(section_parts, 'row')  32.8 us
    reduce_scatter x1, waiting for transfers between devices, per_device(): lax.psum_scatter(section_part, 'row', scatter_dimension=1, tiled=True)  18.6 us
  transfers between devices with their start and end apart: 11, of which 11 were waited for; matrix products, arithmetic and copies ran while one was open for 0% of the time, Pallas kernels for 0%

commit v1 on v0

--- a/solution.py
+++ b/solution.py
@@ -36,7 +36,14 @@
         known_part = sep_rhs[level] - reduced[level]
         if level > 0:
             known_part = known_part - dot_last(y_full, sep_coupling[level - 1])
-        known_full = lax.all_gather(known_part, "leaf", axis=1, tiled=True)
+        ways, here = (lax.axis_size("leaf"), lax.axis_index("leaf"))
+        known_full, reach = (known_part, 1)
+        while reach < ways:
+            theirs = lax.ppermute(known_full, "leaf", [(d, d ^ reach) for d in range(ways)])
+            mine_first = jnp.concatenate([known_full, theirs], axis=1)
+            theirs_first = jnp.concatenate([theirs, known_full], axis=1)
+            known_full = jnp.where(here & reach == 0, mine_first, theirs_first)
+            reach = 2 * reach
         y_level = dot_last(known_full, sep_inverse[level])
         y_leaf.append(y_level)
         if level < levels - 1:

time: 812 us -> 753 us (0.927)
  blocking collectives: 229 us -> 105 us
  waiting for transfers between devices: 535 us -> 586 us
  starting transfers between devices: 0.45 us -> 11.3 us
    all_gather x4 -> x0, blocking collectives: 123 us -> none  [per_device(): known_full = lax.all_gather(known_part, 'leaf', axis=1, tiled=True)]
    ppermute x0 -> x12, waiting for transfers between devices: none -> 51.2 us  [per_device(): lax.ppermute(known_full, 'leaf', [(d, d ^ reach) for d in range(ways)])]
    ppermute x0 -> x12, starting transfers between devices: none -> 10.9 us  [per_device(): lax.ppermute(known_full, 'leaf', [(d, d ^ reach) for d in range(ways)])]
  transfers between devices with their start and end apart: 11 -> 23, of which waited for: 11 -> 23; matrix products, arithmetic and copies ran while one was open for 0% -> 0% of each run, Pallas kernels for 0% -> 0%
where the time goes in v1:
time: 753 us; the launch traced here: 752 us
  waiting for transfers between devices  586 us (78%)
  blocking collectives  105 us (14%)
  matrix products  32.6 us (4%)
  between operations  14 us (2%)
  starting transfers between devices  11.3 us (2%)
    reduce_scatter x4, waiting for transfers between devices, per_device(): lax.psum_scatter(solve_part, 'leaf', scatter_dimension=1, tiled=True)  216 us
    reduce_scatter x3, waiting for transfers between devices, per_device(): lax.psum_scatter(coupling_part, 'leaf', scatter_dimension=1, tiled=True)  163 us
    all_gather x3, blocking collectives, per_device(): y_full = lax.all_gather(y_level, 'leaf', axis=1, tiled=True)  92.7 us
    reduce_scatter x1, waiting for transfers between devices, per_device(): lax.psum_scatter(row_total, 'leaf', scatter_dimension=2, tiled=True)  65.5 us
    ppermute x12, waiting for transfers between devices, per_device(): lax.ppermute(known_full, 'leaf', [(d, d ^ reach) for d in range(ways)])  51.2 us
    all_gather x1, waiting for transfers between devices, per_device(): solved_full = lax.all_gather(solved_stack, 'leaf', axis=2, tiled=True)  38.7 us
    psum x1, waiting for transfers between devices, per_device(): row_total = lax.psum(section_parts, 'row')  32.8 us
    reduce_scatter x1, waiting for transfers between devices, per_device(): lax.psum_scatter(section_part, 'row', scatter_dimension=1, tiled=True)  18.6 us
  transfers between devices with their start and end apart: 23, of which 23 were waited for; matrix products, arithmetic and copies ran while one was open for 0% of the time, Pallas kernels for 0%

profile of v1, /device:TPU:0, one launch (start us, length us, event | category | flops | bytes accessed | tf_op | source)
XLA Modules:
  0.0 752.4 jit_solution(203915319454554147)
XLA Ops:
  7.2 6.9 all_gather.18
  14.7 1.3 fusion.87
  16.1 3.4 fusion
  19.5 65.5 %reduce-scatter.26.cloned.1.call-done = f32[4,64,128]{2,1,0:T(8,128)} async-done(((f32[4,64,1024]{2,1,0:T(8,128)}), f32[4,64,128]{2,1,0:T(8,128)}) %reduce-scatter.26.cloned.1.call-update) | async-done | bytes 131088 | tf_op jit(solution)/shard_map/reduce_scatter | solution.py:32
  85.2 32.8 %all-reduce.2.cloned.1.call-done = f32[4,64,128]{2,1,0:T(8,128)} async-done(((f32[4,64,128]{2,1,0:T(8,128)}), f32[4,64,128]{2,1,0:T(8,128)}) %all-reduce.2.cloned.1.call-update) | async-done | bytes 131088 | tf_op jit(solution)/shard_map/psum | solution.py:31
  118.8 1.5 collective-permute-start
  120.3 2.4 collective-permute-done
  122.7 1.6 collective-permute-start.1
  124.3 4.0 collective-permute-done.1
  128.3 2.0 collective-permute-start.2
  130.3 5.1 collective-permute-done.2
  135.4 1.7 fusion.26
  137.1 30.7 %all_gather.19 = f32[64,1024]{1,0:T(8,128)S(1)} all-gather(f32[64,128]{1,0:T(8,128)S(1)} %fusion.26), channel_id=1, replica_groups=mesh['leaf'=8,'row'=4] {'leaf'}, dimensions={1}, use_global_device_ids=true | all-gather | bytes 294912 | tf_op jit(solution)/shard_map/all_gather | solution.py:50
  167.8 1.7 convolution_subtract_fusion.2
  170.4 3.1 collective-permute-done.3
  173.6 4.3 collective-permute-done.4
  178.6 6.2 collective-permute-done.5
  185.5 31.0 %all_gather.20 = f32[64,1024]{1,0:T(8,128)S(1)} all-gather(f32[64,128]{1,0:T(8,128)S(1)} %fusion.19), channel_id=1, replica_groups=mesh['leaf'=8,'row'=4] {'leaf'}, dimensions={1}, use_global_device_ids=true | all-gather | bytes 294912 | tf_op jit(solution)/shard_map/all_gather | solution.py:50
  216.6 1.7 convolution_subtract_fusion.1
  218.3 1.2 collective-permute-start.6
  219.4 2.8 collective-permute-done.6
  222.3 4.3 collective-permute-done.7
  227.6 6.0 collective-permute-done.8
  234.2 31.0 %all_gather.21 = f32[64,1024]{1,0:T(8,128)S(1)} all-gather(f32[64,128]{1,0:T(8,128)S(1)} %fusion.12), channel_id=1, replica_groups=mesh['leaf'=8,'row'=4] {'leaf'}, dimensions={1}, use_global_device_ids=true | all-gather | bytes 294912 | tf_op jit(solution)/shard_map/all_gather | solution.py:50
  265.2 1.7 convolution_subtract_fusion
  266.9 1.1 collective-permute-start.9
  268.0 2.9 collective-permute-done.9
  271.0 4.3 collective-permute-done.10
  276.1 5.9 collective-permute-done.11
  282.0 1.7 fusion.5
  283.7 2.0 fusion.3
  285.9 53.3 %reduce-scatter.10.cloned.1.call-done = f32[16,128]{1,0:T(8,128)} async-done(((f32[16,1024]{1,0:T(8,128)}), f32[16,128]{1,0:T(8,128)}) %reduce-scatter.10.cloned.1.call-update) | async-done | bytes 8208 | tf_op jit(solution)/shard_map/reduce_scatter | solution.py:62
  339.2 2.1 fusion.7
  341.3 54.2 %reduce-scatter.12.cloned.1.call-done = f32[16,128]{1,0:T(8,128)} async-done(((f32[16,1024]{1,0:T(8,128)}), f32[16,128]{1,0:T(8,128)}) %reduce-scatter.12.cloned.1.call-update) | async-done | bytes 8208 | tf_op jit(solution)/shard_map/reduce_scatter | solution.py:58
  395.5 2.1 fusion.10
  397.6 54.2 %reduce-scatter.14.cloned.1.call-done = f32[16,128]{1,0:T(8,128)} async-done(((f32[16,1024]{1,0:T(8,128)}), f32[16,128]{1,0:T(8,128)}) %reduce-scatter.14.cloned.1.call-update) | async-done | bytes 8208 | tf_op jit(solution)/shard_map/reduce_scatter | solution.py:62
  451.8 2.1 fusion.14
  453.9 54.2 %reduce-scatter.16.cloned.1.call-done = f32[16,128]{1,0:T(8,128)} async-done(((f32[16,1024]{1,0:T(8,128)}), f32[16,128]{1,0:T(8,128)}) %reduce-scatter.16.cloned.1.call-update) | async-done | bytes 8208 | tf_op jit(solution)/shard_map/reduce_scatter | solution.py:58
  508.1 2.1 fusion.17
  510.2 54.3 %reduce-scatter.18.cloned.1.call-done = f32[16,128]{1,0:T(8,128)} async-done(((f32[16,1024]{1,0:T(8,128)}), f32[16,128]{1,0:T(8,128)}) %reduce-scatter.18.cloned.1.call-update) | async-done | bytes 8208 | tf_op jit(solution)/shard_map/reduce_scatter | solution.py:62
  564.6 2.1 fusion.21
  566.7 54.3 %reduce-scatter.20.cloned.1.call-done = f32[16,128]{1,0:T(8,128)} async-done(((f32[16,1024]{1,0:T(8,128)}), f32[16,128]{1,0:T(8,128)}) %reduce-scatter.20.cloned.1.call-update) | async-done | bytes 8208 | tf_op jit(solution)/shard_map/reduce_scatter | solution.py:58
  621.0 2.1 fusion.24
  623.1 54.4 %reduce-scatter.22.cloned.1.call-done = f32[16,128]{1,0:T(8,128)} async-done(((f32[16,1024]{1,0:T(8,128)}), f32[16,128]{1,0:T(8,128)}) %reduce-scatter.22.cloned.1.call-update) | async-done | bytes 8208 | tf_op jit(solution)/shard_map/reduce_scatter | solution.py:62
  678.2 5.9 all_gather.22
  684.2 38.7 %all-gather.2.cloned.1.call-done = f32[4,64,1024]{2,1,0:T(8,128)} async-done(((f32[4,64,128]{2,1,0:T(8,128)}), f32[4,64,1024]{2,1,0:T(8,128)}) %all-gather.2.cloned.1.call-update) | async-done | bytes 1048592 | tf_op jit(solution)/shard_map/all_gather | solution.py:64
  722.9 2.7 fusion.1
  726.6 18.6 %reduce-scatter.24.cloned.1.call-done = f32[64,128]{1,0:T(8,128)} async-done(((f32[64,512]{1,0:T(8,128)}), f32[64,128]{1,0:T(8,128)}) %reduce-scatter.24.cloned.1.call-update) | async-done | bytes 32784 | tf_op jit(solution)/shard_map/reduce_scatter | solution.py:68
  (60 shorter events, 9.5 us)
Async XLA Ops:
  7.2 8.9 %copy-start = (f32[4,1024,128]{2,1,0:T(8,128)S(1)}, f32[4,1024,128]{2,1,0:T(8,128)}, u32[]{:S(2)}) copy-start(f32[4,1024,128]{2,1,0:T(8,128)} %param.12) | copy-start | bytes 6291460
  7.2 77.9 %reduce-scatter.26.cloned.1.call-start = ((), (), s32[]{:S(2)}) async-start(), calls=%async_computation.18 | async-start | bytes 1179648 | tf_op jit(solution)/shard_map/reduce_scatter | solution.py:32
  16.1 101.9 %copy-start.4 = (f32[4,64,128]{2,1,0:T(8,128)S(1)}, f32[4,64,128]{2,1,0:T(8,128)}, u32[]{:S(2)}) copy-start(f32[4,64,128]{2,1,0:T(8,128)} %param.9) | copy-start | bytes 393220
  19.5 98.5 %all-reduce.2.cloned.1.call-start = ((), (), s32[]{:S(2)}) async-start(), calls=%async_computation.19 | async-start | bytes 262144 | tf_op jit(solution)/shard_map/psum | solution.py:31
  85.1 254.0 %reduce-scatter.10.cloned.1.call-start = ((), (), s32[]{:S(2)}) async-start(), calls=%async_computation.9 | async-start | bytes 73728 | tf_op jit(solution)/shard_map/reduce_scatter | solution.py:62
  118.0 98.6 %copy-start.5 = (f32[4,64,128]{2,1,0:T(8,128)S(1)}, f32[4,64,128]{2,1,0:T(8,128)}, u32[]{:S(2)}) copy-start(f32[4,64,128]{2,1,0:T(8,128)} %all-reduce.2.cloned.1.call-done) | copy-start | bytes 393220
  118.8 3.9 collective-permute-start
  122.7 5.5 collective-permute-start.1
  128.3 7.1 collective-permute-start.2
  130.3 54.6 %copy-start.1 = (f32[4,128,1024]{2,1,0:T(8,128)S(1)}, f32[4,128,1024]{2,1,0:T(8,128)}, u32[]{:S(2)}) copy-start(f32[4,128,1024]{2,1,0:T(8,128)} %param.10) | copy-start | bytes 6291460
  169.5 4.0 collective-permute-start.3
  173.5 4.3 collective-permute-start.4
  177.9 7.0 collective-permute-start.5
  218.3 4.0 collective-permute-start.6
  222.3 4.3 collective-permute-start.7
  226.6 7.0 collective-permute-start.8
  266.9 4.0 collective-permute-start.9
  270.9 4.3 collective-permute-start.10
  275.2 6.8 collective-permute-start.11
  285.8 109.7 %reduce-scatter.12.cloned.1.call-start = ((), (), s32[]{:S(2)}) async-start(), calls=%async_computation.10 | async-start | bytes 73728 | tf_op jit(solution)/shard_map/reduce_scatter | solution.py:58
  339.2 338.4 %copy-start.6 = (f32[16,128]{1,0:T(8,128)S(1)}, f32[16,128]{1,0:T(8,128)}, u32[]{:S(2)}) copy-start(f32[16,128]{1,0:T(8,128)} %reduce-scatter.10.cloned.1.call-done) | copy-start | bytes 24580
  341.3 110.5 %reduce-scatter.14.cloned.1.call-start = ((), (), s32[]{:S(2)}) async-start(), calls=%async_computation.11 | async-start | bytes 73728 | tf_op jit(solution)/shard_map/reduce_scatter | solution.py:62
  397.6 110.5 %reduce-scatter.16.cloned.1.call-start = ((), (), s32[]{:S(2)}) async-start(), calls=%async_computation.12 | async-start | bytes 73728 | tf_op jit(solution)/shard_map/reduce_scatter | solution.py:58
  451.8 225.7 %copy-start.7 = (f32[16,128]{1,0:T(8,128)S(1)}, f32[16,128]{1,0:T(8,128)}, u32[]{:S(2)}) copy-start(f32[16,128]{1,0:T(8,128)} %reduce-scatter.14.cloned.1.call-done) | copy-start | bytes 24580
  453.9 110.7 %reduce-scatter.18.cloned.1.call-start = ((), (), s32[]{:S(2)}) async-start(), calls=%async_computation.13 | async-start | bytes 73728 | tf_op jit(solution)/shard_map/reduce_scatter | solution.py:62
  510.2 110.8 %reduce-scatter.20.cloned.1.call-start = ((), (), s32[]{:S(2)}) async-start(), calls=%async_computation.14 | async-start | bytes 73728 | tf_op jit(solution)/shard_map/reduce_scatter | solution.py:58
  566.6 159.0 %copy-start.3 = (f32[128,512]{1,0:T(8,128)S(1)}, f32[128,512]{1,0:T(8,128)}, u32[]{:S(2)}) copy-start(f32[128,512]{1,0:T(8,128)} %param.8) | copy-start | bytes 786436
  566.6 110.9 %reduce-scatter.22.cloned.1.call-start = ((), (), s32[]{:S(2)}) async-start(), calls=%async_computation.15 | async-start | bytes 73728 | tf_op jit(solution)/shard_map/reduce_scatter | solution.py:62
  623.1 99.8 %all-gather.2.cloned.1.call-start = ((), (), s32[]{:S(2)}) async-start(), calls=%async_computation.16 | async-start | bytes 1179648 | tf_op jit(solution)/shard_map/all_gather | solution.py:64
  684.1 61.1 %copy-start.2 = (f32[4,64,128]{2,1,0:T(8,128)S(1)}, f32[4,64,128]{2,1,0:T(8,128)}, u32[]{:S(2)}) copy-start(f32[4,64,128]{2,1,0:T(8,128)} %all_gather.22) | copy-start | bytes 393220
  684.2 61.0 %reduce-scatter.24.cloned.1.call-start = ((), (), s32[]{:S(2)}) async-start(), calls=%async_computation.17 | async-start | bytes 163840 | tf_op jit(solution)/shard_map/reduce_scatter | solution.py:68
Sparse Core Ops, SparseCore 0:
  19.6 65.4 reduce-scatter.25
  87.5 30.4 all-reduce.1
  285.9 53.1 reduce-scatter.9
  342.7 52.7 reduce-scatter.11
  399.0 52.7 reduce-scatter.13
  455.3 52.7 reduce-scatter.15
  511.8 52.7 reduce-scatter.17
  568.3 52.7 reduce-scatter.19
  624.7 52.7 reduce-scatter.21
  684.3 38.5 all-gather.1
  726.7 18.4 reduce-scatter.23
